TPU v7x, 32 devices: a whole 2x2x4 slice. The times are simulated.
32 devices in a mesh: prompt: 8 (over y, x, core), resp: 4 (over z).
Axes of the slice: x: 2, y: 2, z: 4, core: 2. Of those that a mesh axis runs over, the one named last changes fastest.
Arguments:
- hidden_states: bfloat16 [8, 4, 256, 8192], P('prompt', 'resp'), may hold values from -6 to 6
- queries: bfloat16 [8, 4, 256, 1024], P('prompt', 'resp'), may hold values from -100 to 100
- prefix_kv: bfloat16 [8, 512, 256], P('prompt', 'resp'), may hold values from -4 to 4
- kv_weight: bfloat16 [8192, 256], replicated, may hold values from -0.0625 to 0.0625
- out_grad: bfloat16 [8, 4, 256, 1024], P('prompt', 'resp'), may hold values from -6 to 6
- lengths: int32 [8, 4], P('prompt', 'resp'), may hold values from 128 to 256, as said below
- rewards: int32 [8, 4], P('prompt', 'resp'), may hold values from 0 to 3
Outputs:
- attn_out: float32 [8, 4, 256, 1024], P('prompt', 'resp')
- grad_queries: float32 [8, 4, 256, 1024], P('prompt', 'resp')
- grad_prefix_kv: float32 [8, 512, 256], P('prompt', 'resp')
- grad_kv_weight: float32 [8192, 256], P(('prompt', 'resp'))
Inputs may be any that keep to these rules, and one draw needn't show every extreme that they name: `lengths`: every length is a multiple of 16, and in every prompt some response has all 256 positions live.
All inputs are finite; a program needn't handle non-finite values.
Results may differ from a plain program's by a relative error of at most 0.029.
Values may be sent and summed in bfloat16 or wider, within the bound.
A program may use at most 128 MiB of HBM per device.

v0:
```python
import math

import jax
import jax.numpy as jnp
from jax import lax
from jax.sharding import PartitionSpec as P


def on_device(hidden_states, queries, prefix_kv, kv_weight, out_grad, lengths, rewards):
    tokens = hidden_states[0, 0]
    row_count = tokens.shape[0]
    head_width = kv_weight.shape[1] // 2
    head_count = queries.shape[3] // head_width
    flat_rows = row_count * head_count
    gathered = lax.all_gather(prefix_kv, "resp", axis=1, tiled=True)[0]
    prefix_len = gathered.shape[0]
    kv_resp = jnp.dot(tokens, kv_weight, preferred_element_type=jnp.float32).astype(jnp.bfloat16)
    joined_kv = jnp.concatenate([gathered, kv_resp], axis=0)
    key_rows = joined_kv[:, :head_width]
    value_rows = joined_kv[:, head_width:]
    query_rows = queries[0, 0].reshape(flat_rows, head_width)
    length = lengths[0, 0]
    reward = rewards[0, 0].astype(jnp.float32)
    sum_reward, squares, total_len = lax.psum(
        (reward, reward * reward, length.astype(jnp.float32)), "resp"
    )
    samples = lax.axis_size("resp")
    group_mean = sum_reward / samples
    spread = jnp.sqrt(jnp.maximum(squares / samples - group_mean * group_mean, 0.0))
    advantage = (reward - group_mean) / jnp.maximum(spread, 1.0)
    loss_weight = -advantage * (row_count * samples) / total_len
    position = lax.broadcasted_iota(jnp.int32, (flat_rows, 1), 0) // head_count
    key_pos = lax.broadcasted_iota(jnp.int32, (1, row_count), 1)
    allowed = jnp.concatenate(
        [jnp.ones((flat_rows, prefix_len), dtype=bool), (key_pos <= position) & (key_pos < length)],
        axis=1,
    )
    softmax_scale = 1.0 / math.sqrt(head_width)
    contract_last = (((1,), (1,)), ((), ()))
    contract_first = (((0,), (0,)), ((), ()))
    scores = (
        lax.dot_general(query_rows, key_rows, contract_last, preferred_element_type=jnp.float32)
        * softmax_scale
    )
    scores = jnp.where(allowed, scores, -jnp.inf)
    row_max = jnp.max(scores, axis=1, keepdims=True)
    log_total = row_max + jnp.log(jnp.sum(jnp.exp(scores - row_max), axis=1, keepdims=True))
    probs_full = jnp.exp(scores - log_total)
    probs = probs_full.astype(jnp.bfloat16)
    attended_full = jnp.dot(probs, value_rows, preferred_element_type=jnp.float32)
    attended = attended_full.astype(jnp.bfloat16)
    in_range = lax.broadcasted_iota(jnp.int32, (row_count, 1), 0) < length
    cotangent = jnp.where(in_range, loss_weight * out_grad[0, 0].astype(jnp.float32), 0.0).astype(
        jnp.bfloat16
    )
    cotangent = cotangent.reshape(flat_rows, head_width)
    row_delta = jnp.sum(
        cotangent.astype(jnp.float32) * attended.astype(jnp.float32), axis=1, keepdims=True
    )
    grad_probs = lax.dot_general(
        cotangent, value_rows, contract_last, preferred_element_type=jnp.float32
    )
    grad_scores = (probs_full * (grad_probs - row_delta) * softmax_scale).astype(jnp.bfloat16)
    grad_query = jnp.dot(grad_scores, key_rows, preferred_element_type=jnp.float32)

    def key_grads(first_row, num_rows):
        score_cols = lax.dynamic_slice_in_dim(grad_scores, first_row, num_rows, 1)
        prob_cols = lax.dynamic_slice_in_dim(probs, first_row, num_rows, 1)
        key_grad = lax.dot_general(
            score_cols, query_rows, contract_first, preferred_element_type=jnp.float32
        )
        value_grad = lax.dot_general(
            prob_cols, cotangent, contract_first, preferred_element_type=jnp.float32
        )
        return jnp.concatenate([key_grad, value_grad], axis=1)

    prefix_grad = lax.psum_scatter(
        key_grads(jnp.int32(0), prefix_len // samples * lax.axis_size("resp")),
        "resp",
        scatter_dimension=0,
        tiled=True,
    )
    resp_grad = key_grads(prefix_len, row_count).astype(jnp.bfloat16)
    grad_kv_weight = lax.psum_scatter(
        lax.dot_general(tokens, resp_grad, contract_first, preferred_element_type=jnp.float32),
        ("prompt", "resp"),
        scatter_dimension=0,
        tiled=True,
    )
    attn_out = attended_full.reshape(1, 1, row_count, head_count * head_width)
    grad_queries = grad_query.reshape(1, 1, row_count, head_count * head_width)
    return (attn_out, grad_queries, prefix_grad[None], grad_kv_weight)


def solution(mesh):
    placed = (
        P("prompt", "resp", None, None),
        P("prompt", "resp", None, None),
        P("prompt", "resp", None),
        P(),
        P("prompt", "resp", None, None),
        P("prompt", "resp"),
        P("prompt", "resp"),
    )
    return jax.shard_map(
        on_device,
        mesh=mesh,
        in_specs=placed,
        out_specs=(
            P("prompt", "resp", None, None),
            P("prompt", "resp", None, None),
            P("prompt", "resp", None),
            P(("prompt", "resp"), None),
        ),
        check_vma=False,
    )
```

profile of v0, /device:TPU:0, one launch (start us, length us, event | category | flops | bytes accessed | tf_op | source)
XLA Modules:
  0.0 274.3 jit_solution(5895924400696766568)
XLA Ops:
  8.6 14.5 %all-reduce.1 = (f32[]{:T(128)}, f32[]{:T(128)}, f32[]{:T(128)}) all-reduce(f32[]{:T(128)} %bitcast.4, f32[]{:T(128)S(6)} %mul.38, f32[]{:T(128)S(6)} %convert_element_type.41), channel_id=1, replica_groups=mesh['prompt'=8,'resp'=4] {'resp'}, use_global_device_ids=true, to_apply=%region_2.0 | all-reduce | flops 3 | bytes 24 | tf_op jit(solution)/shard_map/psum | solution.py:24
  26.0 14.1 %all_gather.3 = bf16[1,512,256]{2,1,0:T(8,128)(2,1)S(1)} all-gather(bf16[1,128,256]{2,1,0:T(8,128)(2,1)} %param.9), channel_id=1, replica_groups=mesh['prompt'=8,'resp'=4] {'resp'}, dimensions={1}, use_global_device_ids=true | all-gather | bytes 327680 | tf_op jit(solution)/shard_map/all_gather | solution.py:15
  41.1 1.1 convert_multiply_fusion
  42.5 1.0 copy.15
  43.8 4.9 %fusion.9 = bf16[256,256]{1,0:T(8,128)(2,1)S(1)} fusion(bf16[8192,256]{1,0:T(8,128)(2,1)} %param.10, bf16[1,1,256,8192]{3,2,1,0:T(8,128)(2,1)} %param.7), kind=kOutput, calls=%fused_computation.15 | convolution fusion | flops 1073807360 | bytes 8519680 | tf_op jit(solution)/shard_map/dot_general | solution.py:17
  48.7 1.0 fusion.28
  49.7 0.9 exponential_reduce_fusion
  50.6 0.9 fusion
  51.6 1.6 multiply_reduce_fusion
  53.3 0.8 fusion.4
  54.1 1.6 multiply_convert_fusion
  55.7 1.7 copy-done
  58.3 0.8 pad_maximum_fusion
  59.4 1.8 convolution_convert_fusion.1
  61.2 1.5 convolution_convert_fusion
  62.7 6.8 %convolution_bitcast_fusion = f32[8192,256]{0,1:T(8,128)} fusion(bf16[1,1,256,8192]{3,2,1,0:T(8,128)(2,1)} %param.7, bf16[256,128]{1,0:T(8,128)(2,1)S(1)} %convolution_convert_fusion, bf16[256,128]{1,0:T(8,128)(2,1)S(1)} %convolution_convert_fusion.1), kind=kOutput, calls=%fused_computation | convolution fusion | flops 1074003968 | bytes 12713984 | tf_op jit(solution)/shard_map/dot_general | solution.py:85
  69.5 1.9 copy-done.1
  71.4 2.1 fusion.25
  73.5 2.4 reshape.79
  75.8 1.5 copy.14
  77.4 1.1 reshape.78
  79.3 1.7 copy.17
  80.9 184.7 %reduce-scatter.5.cloned.1.call-done = f32[256,256]{0,1:T(8,128)} async-done(((f32[8192,256]{0,1:T(8,128)}), f32[256,256]{0,1:T(8,128)}) %reduce-scatter.5.cloned.1.call-update) | async-done | bytes 262160 | tf_op jit(solution)/shard_map/reduce_scatter | solution.py:84
  265.6 1.8 copy.18
  (26 shorter events, 3.1 us)
Async XLA Ops:
  7.2 36.4 %copy-start.4 = (bf16[1,1,256,1024]{3,2,1,0:T(8,128)(2,1)S(1)}, bf16[1,1,256,1024]{3,2,1,0:T(8,128)(2,1)}, u32[]{:S(2)}) copy-start(bf16[1,1,256,1024]{3,2,1,0:T(8,128)(2,1)} %param.8) | copy-start | bytes 1572868
  7.2 72.1 %reduce-scatter.3.cloned.1.call-start = ((), (), s32[]{:S(2)}) async-start(), calls=%async_computation.2 | async-start | bytes 655360 | tf_op jit(solution)/shard_map/reduce_scatter | solution.py:77
  43.7 4.9 %copy-start.5 = (bf16[2048,128]{1,0:T(8,128)(2,1)}, bf16[2048,128]{1,0:T(8,128)(2,1)S(1)}, u32[]{:S(2)}) copy-start(bf16[2048,128]{1,0:T(8,128)(2,1)S(1)} %reshape_squeeze.3) | copy-start | bytes 1572868
  50.6 1.0 copy-start.3
  53.2 2.5 copy-start.2
  54.1 3.4 %copy-start.6 = (bf16[2048,128]{1,0:T(8,128)(2,1)S(1)}, bf16[2048,128]{1,0:T(8,128)(2,1)}, u32[]{:S(2)}) copy-start(bf16[2048,128]{1,0:T(8,128)(2,1)} %copy-done.5) | copy-start | bytes 1572868
  55.7 1.8 copy-start
  59.2 206.5 %reduce-scatter.5.cloned.1.call-start = ((), (), s32[]{:S(2)}) async-start(), calls=%async_computation.3 | async-start | bytes 8650752 | tf_op jit(solution)/shard_map/reduce_scatter | solution.py:84
  69.5 1.9 copy-start.1
Sparse Core Ops, SparseCore 0:
  59.3 19.9 reduce-scatter.2
  81.6 184.0 reduce-scatter.4
where the time goes:
time: 275 us; the launch traced here: 274 us
  waiting for transfers between devices  185 us (67%)
  blocking collectives  28.6 us (10%)
  matrix products  22.9 us (8%)
  between operations  18.9 us (7%)
  local copies, waits for them, and re-layouts  13.9 us (5%)
  other arithmetic  4.2 us (2%)
    reduce_scatter x1, waiting for transfers between devices, on_device(): lax.psum_scatter(lax.dot_general(tokens, resp_grad, contract_first, prefe...  185 us
    psum x1, blocking collectives, on_device(): lax.psum((reward, reward * reward, length.astype(jnp.float32)), 'resp')  14.5 us
    all_gather x1, blocking collectives, on_device(): gathered = lax.all_gather(prefix_kv, 'resp', axis=1, tiled=True)[0]  14.1 us
    unnamed x16, local copies, waits for them, and re-layouts  7.18 us
    dot_general x1, matrix products, on_device(): lax.dot_general(tokens, resp_grad, contract_first, preferred_element_type...  6.79 us
  transfers between devices with their start and end apart: 2, of which 2 were waited for; matrix products, arithmetic and copies ran while one was open for 7% of the time, Pallas kernels for 0%

commit v1 on v0

v1 whole, which is shorter than its diff:
```python
import math

import jax
import jax.numpy as jnp
from jax import lax
from jax.experimental import pallas as pl
from jax.experimental.pallas import tpu as pltpu
from jax.sharding import PartitionSpec as P

F32 = jnp.float32
BF16 = jnp.bfloat16
MESH = pl.DeviceIdType.MESH
NT = (((1,), (1,)), ((), ()))
TN = (((0,), (0,)), ((), ()))


def flip(value, mask):
    out = value
    bit = 0
    while (1 << bit) <= mask:
        if (mask >> bit) & 1:
            out = out + (1 - 2 * ((value // (1 << bit)) % 2)) * (1 << bit)
        bit += 1
    return out


def make_kernel(prompts, samples, rows, heads, hd, shard, model):
    bits = (prompts // 2).bit_length() - 1
    half = prompts // 2
    chunk = model // prompts
    block = chunk // samples
    prefix = shard * samples
    scale = 1.0 / math.sqrt(hd)
    log2e = 1.0 / math.log(2.0)
    stepwise = block % 128 == 0
    orders = (list(range(bits)), list(reversed(range(bits))))

    def kernel(
        hidden, queries, prefix_in, weight, out_grad, lengths, rewards,
        attn_out, grad_queries, grad_prefix, grad_weight,
        hid, hid_other, wgt, qry, gout, kv, kv_t, stats,
        attn_v, gq_v, acc, prefix_send, prefix_recv, resp_grad, grads, z_recv, *rest,
    ):
        recv_bufs = (rest[:bits], rest[bits:2 * bits])
        (load_sem, out_sem, hx_send, hx_recv, gather_send, gather_recv, stat_send, stat_recv,
         own_sem, rg_send, rg_recv, ps_send, ps_recv, red_send, red_recv, z_send, z_recv_sem) = rest[2 * bits:]
        p = lax.axis_index("prompt")
        z = lax.axis_index("resp")
        core = p % 2
        high = p // 2
        my_bits = [(high // (1 << b)) % 2 for b in range(bits)]
        partner = {"prompt": flip(p, 1)}
        bit_peer = [{"prompt": flip(p, 2 << b)} for b in range(bits)]
        z_of = [flip(z, k) for k in range(samples)]
        z_peer = [{"resp": z_of[k]} for k in range(samples)]

        hid_loads, wgt_loads = [], []
        for j in range(prompts):
            cols = pl.ds(j * chunk, chunk)
            a = pltpu.make_async_copy(hidden.at[0, 0, :, cols], hid.at[j], load_sem.at[j])
            b = pltpu.make_async_copy(weight.at[cols], wgt.at[j], load_sem.at[prompts + j])
            a.start()
            b.start()
            hid_loads.append(a)
            wgt_loads.append(b)
        q_load = pltpu.make_async_copy(queries.at[0, 0], qry, load_sem.at[2 * prompts])
        g_load = pltpu.make_async_copy(out_grad.at[0, 0], gout, load_sem.at[2 * prompts + 1])
        own_rows = pl.ds(pl.multiple_of(z * shard, shard), shard)
        own_prefix = pltpu.make_async_copy(prefix_in.at[0], kv.at[own_rows], own_sem)
        own_prefix.start()
        q_load.start()
        g_load.start()

        row_id = lax.broadcasted_iota(jnp.int32, (8, 128), 0)
        length = lengths[0, 0]
        mine = jnp.where(row_id == 0, rewards[0, 0].astype(F32), length.astype(F32))
        stats[0] = mine

        barrier = pltpu.get_barrier_semaphore()
        peers = [partner] + bit_peer + z_peer[1:]
        for peer in peers:
            pl.semaphore_signal(barrier, inc=1, device_id=peer, device_id_type=MESH)
        pl.semaphore_wait(barrier, len(peers))

        def remote(src, dst, ssem, rsem, peer):
            return pltpu.make_async_remote_copy(
                src_ref=src, dst_ref=dst, send_sem=ssem, recv_sem=rsem,
                device_id=peer, device_id_type=MESH,
            )

        gathers, stat_copies = [], []
        for k in range(samples - 1, 0, -1):
            g = remote(prefix_in.at[0], kv.at[own_rows], gather_send.at[k], gather_recv.at[k], z_peer[k])
            s = remote(stats.at[0], stats.at[k], stat_send.at[k], stat_recv.at[k], z_peer[k])
            g.start()
            s.start()
            gathers.append(g)
            stat_copies.append(s)
        swaps = []
        for j in range(half):
            cols = pl.ds(pl.multiple_of((2 * j + 1 - core) * chunk, chunk), chunk)
            c = remote(hidden.at[0, 0, :, cols], hid_other.at[j], hx_send.at[j], hx_recv.at[j], partner)
            c.start()
            swaps.append(c)

        total = jnp.zeros((rows, 2 * hd), F32)
        for j in range(prompts):
            hid_loads[j].wait()
            wgt_loads[j].wait()
            total = total + jnp.dot(hid[j], wgt[j], preferred_element_type=F32)
        kv[prefix:, :] = total.astype(BF16)

        for s in stat_copies:
            s.wait()
        reward_sum = mine
        for k in range(1, samples):
            reward_sum = reward_sum + stats[k]
        mean = reward_sum[0:1, :] / samples
        square = jnp.zeros((1, 128), F32)
        for k in range(samples):
            d = stats[k][0:1, :] - mean
            square = square + d * d
        spread = jnp.sqrt(square / samples)
        advantage = (mine[0:1, :] - mean) / jnp.maximum(spread, 1.0)
        loss_weight = -advantage * (rows * samples) / reward_sum[1:2, :]

        own_prefix.wait()
        for g in gathers:
            g.wait()
        kv_t[...] = kv[...].astype(F32).T.astype(BF16)
        acc[...] = jnp.zeros_like(acc)
        q_load.wait()
        g_load.wait()

        live = lax.broadcasted_iota(jnp.int32, (rows, hd), 0) < length
        key_id = lax.broadcasted_iota(jnp.int32, (rows, rows), 0)
        time_id = lax.broadcasted_iota(jnp.int32, (rows, rows), 1)
        allowed = (key_id <= time_id) & (key_id < length)

        def head(h, carry):
            cols = pl.ds(pl.multiple_of(h * hd, hd), hd)
            q = qry[:, cols]
            cot32 = jnp.where(live, gout[:, cols].astype(F32) * loss_weight, 0.0)
            cot = cot32.astype(BF16)
            cot_t32 = cot.astype(F32).T
            cot_t = cot_t32.astype(BF16)
            s_pre = lax.dot_general(kv[:prefix, :hd], q, NT, preferred_element_type=F32) * (scale * log2e)
            s_res = lax.dot_general(kv[prefix:, :hd], q, NT, preferred_element_type=F32) * (scale * log2e)
            s_res = jnp.where(allowed, s_res, -jnp.inf)
            top = jnp.maximum(jnp.max(s_pre, axis=0, keepdims=True), jnp.max(s_res, axis=0, keepdims=True))
            e_pre = jnp.exp2(s_pre - top)
            e_res = jnp.exp2(s_res - top)
            inv = 1.0 / (jnp.sum(e_pre, axis=0, keepdims=True) + jnp.sum(e_res, axis=0, keepdims=True))
            f_pre = e_pre * inv
            f_res = e_res * inv
            p_pre = f_pre.astype(BF16)
            p_res = f_res.astype(BF16)
            out_t = jnp.dot(kv_t[hd:, :prefix], p_pre, preferred_element_type=F32) + jnp.dot(
                kv_t[hd:, prefix:], p_res, preferred_element_type=F32)
            attn_v[:, cols] = out_t.T
            delta = jnp.sum(cot_t32 * out_t.astype(BF16).astype(F32), axis=0, keepdims=True)
            d_pre = jnp.dot(kv[:prefix, hd:], cot_t, preferred_element_type=F32)
            d_res = jnp.dot(kv[prefix:, hd:], cot_t, preferred_element_type=F32)
            gs_pre = (f_pre * (d_pre - delta)).astype(BF16)
            gs_res = (f_res * (d_res - delta)).astype(BF16)
            gq_t = jnp.dot(kv_t[:hd, :prefix], gs_pre, preferred_element_type=F32) + jnp.dot(
                kv_t[:hd, prefix:], gs_res, preferred_element_type=F32)
            gq_v[:, cols] = (gq_t * scale).T
            acc[:prefix, :hd] += jnp.dot(gs_pre, q, preferred_element_type=F32)
            acc[prefix:, :hd] += jnp.dot(gs_res, q, preferred_element_type=F32)
            acc[:prefix, hd:] += jnp.dot(p_pre, cot, preferred_element_type=F32)
            acc[prefix:, hd:] += jnp.dot(p_res, cot, preferred_element_type=F32)
            return carry

        lax.fori_loop(0, heads, head, 0)

        resp_grad[0, :, :hd] = (acc[prefix:, :hd] * scale).astype(BF16)
        resp_grad[0, :, hd:] = acc[prefix:, hd:].astype(BF16)
        rg = remote(resp_grad.at[0], resp_grad.at[1], rg_send, rg_recv, partner)
        rg.start()
        out_copies = [
            pltpu.make_async_copy(attn_v, attn_out.at[0, 0], out_sem.at[0]),
            pltpu.make_async_copy(gq_v, grad_queries.at[0, 0], out_sem.at[1]),
        ]
        for c in out_copies:
            c.start()
        prefix_send[:, :hd] = (acc[:prefix, :hd] * scale).astype(BF16)
        prefix_send[:, hd:] = acc[:prefix, hd:].astype(BF16)
        prefix_copies = []
        for k in range(samples - 1, 0, -1):
            dest = pl.ds(pl.multiple_of(z_of[k] * shard, shard), shard)
            c = remote(prefix_send.at[dest], prefix_recv.at[k - 1], ps_send.at[k], ps_recv.at[k], z_peer[k])
            c.start()
            prefix_copies.append(c)
        for c in swaps:
            c.wait()
        rg.wait()

        def spot(s, zd, fixed):
            return (s, zd) + tuple(fixed[b] for b in reversed(range(bits)))

        def project(j, cols, width):
            mine_part = lax.dot_general(
                hid[2 * j + core, :, cols], resp_grad[0], TN, preferred_element_type=F32)
            return mine_part + lax.dot_general(
                hid_other[j, :, cols], resp_grad[1], TN, preferred_element_type=F32)

        def static_bits(j):
            return [(j >> b) & 1 for b in range(bits)]

        def produce(k):
            cols = pl.ds(pl.multiple_of(z_of[k] * block, block), block)
            for j in range(half):
                value = project(j, cols, block).astype(BF16)
                for s in range(2):
                    grads[spot(s, z_of[k], static_bits(j))] = value[:, s * hd:(s + 1) * hd]

        if not stepwise:
            for j in range(half):
                value = project(j, pl.ds(0, chunk), chunk).astype(BF16)
                for zd in range(samples):
                    for s in range(2):
                        grads[spot(s, zd, static_bits(j))] = value[zd * block:(zd + 1) * block, s * hd:(s + 1) * hd]

        started = {}

        def kept(s, phase):
            fixed = [slice(None)] * bits
            for b in orders[s][:phase]:
                fixed[b] = my_bits[b]
            return fixed

        def send(k, phase):
            for s in range(2):
                b = orders[s][phase]
                fixed = kept(s, phase)
                fixed[b] = 1 - my_bits[b]
                c = remote(
                    grads.at[spot(s, z_of[k], fixed)], recv_bufs[s][phase].at[k],
                    red_send.at[s, phase, k], red_recv.at[s, phase, k], bit_peer[b])
                c.start()
                started[s, phase, k] = c

        def merge(k, phase):
            for s in range(2):
                started[s, phase, k].wait_recv()
                at = spot(s, z_of[k], kept(s, phase + 1))
                grads[at] = (grads[at].astype(F32) + recv_bufs[s][phase][k].astype(F32)).astype(BF16)

        z_copies = []

        def send_z(k):
            if k == 0:
                return
            for s in range(2):
                c = remote(
                    grads.at[spot(s, z_of[k], my_bits)], z_recv.at[s, k - 1],
                    z_send.at[s, k], z_recv_sem.at[s, k], z_peer[k])
                c.start()
                z_copies.append(c)

        steps = list(range(samples - 1, -1, -1))
        ahead = 1
        for tick in range(samples + ahead + bits):
            if tick < samples:
                if stepwise:
                    produce(steps[tick])
                send(steps[tick], 0)
            for phase in range(bits):
                at = tick - ahead - phase
                if 0 <= at < samples:
                    merge(steps[at], phase)
                    if phase + 1 < bits:
                        send(steps[at], phase + 1)
                    else:
                        send_z(steps[at])

        for c in prefix_copies:
            c.wait()
        own_sum = acc[own_rows, :hd] * scale
        own_val = acc[own_rows, hd:]
        for k in range(samples - 1):
            own_sum = own_sum + prefix_recv[k, :, :hd].astype(F32)
            own_val = own_val + prefix_recv[k, :, hd:].astype(F32)
        grad_prefix[0, :, :hd] = own_sum
        grad_prefix[0, :, hd:] = own_val

        for c in z_copies:
            c.wait()
        for s in range(2):
            value = grads[spot(s, z, my_bits)].astype(F32)
            for k in range(samples - 1):
                value = value + z_recv[s, k].astype(F32)
            grad_weight[:, s * hd:(s + 1) * hd] = value
        for c in started.values():
            c.wait_send()
        for c in out_copies:
            c.wait()

    keys = prefix + rows
    dma = pltpu.SemaphoreType.DMA
    reduce_bufs = [
        pltpu.VMEM((samples,) + (2,) * (bits - 1 - phase) + (block, hd), BF16)
        for _ in range(2) for phase in range(bits)
    ]
    scratch = [
        pltpu.VMEM((prompts, rows, chunk), BF16),
        pltpu.VMEM((half, rows, chunk), BF16),
        pltpu.VMEM((prompts, chunk, 2 * hd), BF16),
        pltpu.VMEM((rows, heads * hd), BF16),
        pltpu.VMEM((rows, heads * hd), BF16),
        pltpu.VMEM((keys, 2 * hd), BF16),
        pltpu.VMEM((2 * hd, keys), BF16),
        pltpu.VMEM((samples, 8, 128), F32),
        pltpu.VMEM((rows, heads * hd), F32),
        pltpu.VMEM((rows, heads * hd), F32),
        pltpu.VMEM((keys, 2 * hd), F32),
        pltpu.VMEM((prefix, 2 * hd), BF16),
        pltpu.VMEM((samples - 1, shard, 2 * hd), BF16),
        pltpu.VMEM((2, rows, 2 * hd), BF16),
        pltpu.VMEM((2, samples) + (2,) * bits + (block, hd), BF16),
        pltpu.VMEM((2, samples - 1, block, hd), BF16),
        *reduce_bufs,
        dma((2 * prompts + 2,)), dma((2,)), dma((half,)), dma((half,)),
        dma((samples,)), dma((samples,)), dma((samples,)), dma((samples,)),
        dma, dma, dma, dma((samples,)), dma((samples,)),
        dma((2, bits, samples)), dma((2, bits, samples)), dma((2, samples)), dma((2, samples)),
    ]
    anywhere = pl.BlockSpec(memory_space=pl.ANY)
    smem = pl.BlockSpec(memory_space=pltpu.SMEM)
    vmem = pl.BlockSpec(memory_space=pltpu.VMEM)
    flops = 4 * rows * model * 2 * hd + 14 * rows * heads * keys * hd
    return pl.pallas_call(
        kernel,
        out_shape=(
            jax.ShapeDtypeStruct((1, 1, rows, heads * hd), F32),
            jax.ShapeDtypeStruct((1, 1, rows, heads * hd), F32),
            jax.ShapeDtypeStruct((1, shard, 2 * hd), F32),
            jax.ShapeDtypeStruct((block, 2 * hd), F32),
        ),
        in_specs=[anywhere] * 5 + [smem] * 2,
        out_specs=(anywhere, anywhere, vmem, vmem),
        scratch_shapes=scratch,
        compiler_params=pltpu.CompilerParams(
            collective_id=0, has_side_effects=True, vmem_limit_bytes=56 * 1024 * 1024),
        cost_estimate=pl.CostEstimate(
            flops=flops, bytes_accessed=16 * 1024 * 1024, transcendentals=rows * heads * keys),
    )


def solution(mesh):
    prompts, samples = mesh.shape["prompt"], mesh.shape["resp"]

    def on_device(hidden, queries, prefix_kv, weight, out_grad, lengths, rewards):
        hd = weight.shape[1] // 2
        call = make_kernel(
            prompts, samples, hidden.shape[2], queries.shape[3] // hd, hd, prefix_kv.shape[1], weight.shape[0])
        return call(hidden, queries, prefix_kv, weight, out_grad, lengths, rewards)

    placed = P("prompt", "resp", None, None)
    return jax.shard_map(
        on_device,
        mesh=mesh,
        in_specs=(placed, placed, P("prompt", "resp", None), P(), placed, P("prompt", "resp"), P("prompt", "resp")),
        out_specs=(placed, placed, P("prompt", "resp", None), P(("prompt", "resp"), None)),
        check_vma=False,
    )
```

time: 275 us -> 57 us (0.21)
  waiting for transfers between devices: 185 us -> 0 us
  Pallas kernels: 0 us -> 48.9 us
  blocking collectives: 28.6 us -> 0 us
  matrix products: 22.9 us -> 0 us
  between operations: 18.9 us -> 1.95 us
  local copies, waits for them, and re-layouts: 13.9 us -> 6.03 us
  other arithmetic: 4.2 us -> 0 us
    reduce_scatter x2 -> x0, waiting for transfers between devices: 185 us -> none  [the longest x1 185 us: on_device(): lax.psum_scatter(lax.dot_general(tokens, resp_grad, contract_first, prefe...]
    pallas_call x0 -> x1, Pallas kernels: none -> 48.9 us  [on_device(): return call(hidden, queries, prefix_kv, weight, out_grad, lengths, rewards)]
    dot_general x10 -> x0, matrix products: 22.9 us -> none  [the longest x1 6.79 us: on_device(): lax.dot_general(tokens, resp_grad, contract_first, preferred_element_type...]
    psum x1 -> x0, blocking collectives: 14.5 us -> none  [on_device(): lax.psum((reward, reward * reward, length.astype(jnp.float32)), 'resp')]
    all_gather x1 -> x0, blocking collectives: 14.1 us -> none  [on_device(): gathered = lax.all_gather(prefix_kv, 'resp', axis=1, tiled=True)[0]]
    reshape x2 -> x0, local copies, waits for them, and re-layouts: 3.49 us -> none  [the longest x1 2.35 us: on_device(): grad_queries = grad_query.reshape(1, 1, row_count, head_count * head_width)]
    unnamed x16 -> x8, local copies, waits for them, and re-layouts: 7.18 us -> 6.03 us
  transfers between devices with their start and end apart: 2 -> 0, of which waited for: 2 -> 0; matrix products, arithmetic and copies ran while one was open for 7% -> 0% of each run, Pallas kernels for 0% -> 0%
where the time goes in v1:
time: 57 us; the launch traced here: 56.8 us
  Pallas kernels  48.9 us (86%)
  local copies, waits for them, and re-layouts  6.03 us (11%)
  between operations  1.95 us (3%)
    pallas_call x1, Pallas kernels, on_device(): return call(hidden, queries, prefix_kv, weight, out_grad, lengths, rewards)  48.9 us
    unnamed x8, local copies, waits for them, and re-layouts  6.03 us

profile of v1, /device:TPU:0, one launch (start us, length us, event | category | flops | bytes accessed | tf_op | source)
XLA Modules:
  0.0 56.8 jit_solution(16727886563888985591)
XLA Ops:
  1.9 48.9 %shard_map.102 = (f32[1,1,256,1024]{3,2,1,0:T(8,128)}, f32[1,1,256,1024]{3,2,1,0:T(8,128)}, f32[1,128,256]{2,1,0:T(8,128)}, f32[256,256]{1,0:T(8,128)}) custom-call(bf16[1,1,256,8192]{3,2,1,0:T(8,128)(2,1)} %hidden.1, bf16[1,1,256,1024]{3,2,1,0:T(8,128)(2,1)} %queries.1, bf16[1,128,256]{2,1,0:T(8,128)(2,1)} %prefix_in.1, bf16[8192,256]{1,0:T(8,128)(2,1)} %weight.1, ...), custom_call_target="tpu_custom_call" | custom-call | flops 4966055936 | bytes 16777216 | tf_op jit(solution)/shard_map/pallas_call | solution.py:358
  50.8 0.0 copy-start.1
  50.8 0.0 copy-start
  50.8 2.4 %copy.17 = f32[1,1,256,1024]{3,2,1,0:T(8,128)} copy(f32[1,1,256,1024]{3,2,1,0:T(8,128)} %get-tuple-element.8) | data formatting | bytes 2097152
  53.2 2.3 %copy.18 = f32[1,1,256,1024]{3,2,1,0:T(8,128)} copy(f32[1,1,256,1024]{3,2,1,0:T(8,128)} %get-tuple-element.9) | data formatting | bytes 2097152
  55.5 0.0 copy-done.1
  55.5 0.7 %copy.19 = f32[1,128,256]{2,1,0:T(8,128)} copy(f32[1,128,256]{2,1,0:T(8,128)S(1)} %copy-done.1) | data formatting | bytes 262144
  56.1 0.0 copy-done
  56.1 0.7 %copy.20 = f32[256,256]{1,0:T(8,128)} copy(f32[256,256]{1,0:T(8,128)S(1)} %copy-done) | data formatting | bytes 524288
Async XLA Ops:
  50.8 4.7 %copy-start.1 = (f32[1,128,256]{2,1,0:T(8,128)S(1)}, f32[1,128,256]{2,1,0:T(8,128)}, u32[]{:S(2)}) copy-start(f32[1,128,256]{2,1,0:T(8,128)} %get-tuple-element.10) | copy-start | bytes 393220
  50.8 5.3 %copy-start = (f32[256,256]{1,0:T(8,128)S(1)}, f32[256,256]{1,0:T(8,128)}, u32[]{:S(2)}) copy-start(f32[256,256]{1,0:T(8,128)} %get-tuple-element.11) | copy-start | bytes 786436

commit v2 on v1

--- a/solution.py
+++ b/solution.py
@@ -172,7 +172,7 @@
             acc[prefix:, hd:] += jnp.dot(p_res, cot, preferred_element_type=F32)
             return carry
 
-        lax.fori_loop(0, heads, head, 0)
+        lax.fori_loop(0, heads, head, 0, unroll=4)
 
         resp_grad[0, :, :hd] = (acc[prefix:, :hd] * scale).astype(BF16)
         resp_grad[0, :, hd:] = acc[prefix:, hd:].astype(BF16)
@@ -348,6 +348,40 @@
     )
 
 
+def hand_out(arrays, pieces=2):
+    def kernel(*refs):
+        count = len(arrays)
+        ins, outs, held, sem = refs[:count], refs[count:2 * count], refs[2 * count:3 * count], refs[3 * count]
+        loads, stores = [], []
+        for i in range(count):
+            axis = len(ins[i].shape) - 2
+            step = ins[i].shape[axis] // pieces
+            for j in range(pieces):
+                at = (0,) * axis + (pl.ds(j * step, step),)
+                loads.append(pltpu.make_async_copy(ins[i].at[at], held[i].at[at], sem.at[0, i, j]))
+                stores.append(pltpu.make_async_copy(held[i].at[at], outs[i].at[at], sem.at[1, i, j]))
+        for c in loads:
+            c.start()
+        for load, store in zip(loads, stores):
+            load.wait()
+            store.start()
+        for c in stores:
+            c.wait()
+
+    anywhere = pl.BlockSpec(memory_space=pl.ANY)
+    size = sum(a.size * 4 for a in arrays)
+    return pl.pallas_call(
+        kernel,
+        out_shape=tuple(jax.ShapeDtypeStruct(a.shape, a.dtype) for a in arrays),
+        in_specs=[anywhere] * len(arrays),
+        out_specs=(anywhere,) * len(arrays),
+        scratch_shapes=[pltpu.VMEM(a.shape, a.dtype) for a in arrays]
+        + [pltpu.SemaphoreType.DMA((2, len(arrays), pieces))],
+        compiler_params=pltpu.CompilerParams(vmem_limit_bytes=60 * 1024 * 1024),
+        cost_estimate=pl.CostEstimate(flops=0, bytes_accessed=2 * size, transcendentals=0),
+    )(*arrays)
+
+
 def solution(mesh):
     prompts, samples = mesh.shape["prompt"], mesh.shape["resp"]
 
@@ -355,7 +389,7 @@
         hd = weight.shape[1] // 2
         call = make_kernel(
             prompts, samples, hidden.shape[2], queries.shape[3] // hd, hd, prefix_kv.shape[1], weight.shape[0])
-        return call(hidden, queries, prefix_kv, weight, out_grad, lengths, rewards)
+        return tuple(hand_out(call(hidden, queries, prefix_kv, weight, out_grad, lengths, rewards)))
 
     placed = P("prompt", "resp", None, None)
     return jax.shard_map(

time: 57 us -> 52.6 us (0.923)
  local copies, waits for them, and re-layouts: 6.03 us -> 0 us
  Pallas kernels: 48.9 us -> 50.5 us
    unnamed x8 -> x0, local copies, waits for them, and re-layouts: 6.03 us -> none
    pallas_call x1 -> x2, Pallas kernels: 48.9 us -> 50.5 us  [the longest x1 47.9 us: on_device(): call(hidden, queries, prefix_kv, weight, out_grad, lengths, rewards)]
where the time goes in v2:
time: 52.6 us; the launch traced here: 52.4 us
  Pallas kernels  50.5 us (96%)
  between operations  1.93 us (4%)
    pallas_call x1, Pallas kernels, on_device(): call(hidden, queries, prefix_kv, weight, out_grad, lengths, rewards)  47.9 us
    pallas_call x1, Pallas kernels, hand_out(): pl.pallas_call(kernel, out_shape=tuple((jax.ShapeDtypeStruct(a.shape, a.d...  2.61 us

profile of v2, /device:TPU:0, one launch (start us, length us, event | category | flops | bytes accessed | tf_op | source)
XLA Modules:
  0.0 52.4 jit_solution(11121706107259235581)
XLA Ops:
  1.9 47.9 %shard_map.102 = (f32[1,1,256,1024]{3,2,1,0:T(8,128)}, f32[1,1,256,1024]{3,2,1,0:T(8,128)}, f32[1,128,256]{2,1,0:T(8,128)}, f32[256,256]{1,0:T(8,128)}) custom-call(bf16[1,1,256,8192]{3,2,1,0:T(8,128)(2,1)} %hidden.1, bf16[1,1,256,1024]{3,2,1,0:T(8,128)(2,1)} %queries.1, bf16[1,128,256]{2,1,0:T(8,128)(2,1)} %prefix_in.1, bf16[8192,256]{1,0:T(8,128)(2,1)} %weight.1, ...), custom_call_target="tpu_custom_call" | custom-call | flops 4966055936 | bytes 16777216 | tf_op jit(solution)/shard_map/pallas_call | solution.py:392
  49.8 2.6 %shard_map.103 = (f32[1,1,256,1024]{3,2,1,0:T(8,128)}, f32[1,1,256,1024]{3,2,1,0:T(8,128)}, f32[1,128,256]{2,1,0:T(8,128)}, f32[256,256]{1,0:T(8,128)}) custom-call(f32[1,1,256,1024]{3,2,1,0:T(8,128)} %get-tuple-element.8.refs_0_, f32[1,1,256,1024]{3,2,1,0:T(8,128)} %get-tuple-element.9.refs_1_, f32[1,128,256]{2,1,0:T(8,128)} %get-tuple-element.10.refs_2_, ...), custom_call_target="tpu_custom_call" | custom-call | bytes 4980736 | tf_op jit(solution)/shard_map/pallas_call | solution.py:373

commit v3 on v2

--- a/solution.py
+++ b/solution.py
@@ -39,7 +39,7 @@
         hidden, queries, prefix_in, weight, out_grad, lengths, rewards,
         attn_out, grad_queries, grad_prefix, grad_weight,
         hid, hid_other, wgt, qry, gout, kv, kv_t, stats,
-        attn_v, gq_v, acc, prefix_send, prefix_recv, resp_grad, grads, z_recv, *rest,
+        attn_v, gq_v, acc, prefix_send, prefix_recv, resp_grad, grads, z_recv, cots_t, own_s, own_d, *rest,
     ):
         recv_bufs = (rest[:bits], rest[bits:2 * bits])
         (load_sem, out_sem, hx_send, hx_recv, gather_send, gather_recv, stat_send, stat_recv,
@@ -124,29 +124,39 @@
         advantage = (mine[0:1, :] - mean) / jnp.maximum(spread, 1.0)
         loss_weight = -advantage * (rows * samples) / reward_sum[1:2, :]
 
+        q_load.wait()
+        g_load.wait()
+
+        live = lax.broadcasted_iota(jnp.int32, (rows, hd), 0) < length
+        key_id = lax.broadcasted_iota(jnp.int32, (rows, rows), 0)
+        time_id = lax.broadcasted_iota(jnp.int32, (rows, rows), 1)
+        allowed = (key_id <= time_id) & (key_id < length)
+
+        def own_scores(h, carry):
+            cols = pl.ds(pl.multiple_of(h * hd, hd), hd)
+            cot = jnp.where(live, gout[:, cols].astype(F32) * loss_weight, 0.0).astype(BF16)
+            cot_t = cot.astype(F32).T.astype(BF16)
+            gout[:, cols] = cot
+            cots_t[h] = cot_t
+            s_res = lax.dot_general(kv[prefix:, :hd], qry[:, cols], NT, preferred_element_type=F32) * (scale * log2e)
+            own_s[h] = jnp.where(allowed, s_res, -jnp.inf)
+            own_d[h] = jnp.dot(kv[prefix:, hd:], cot_t, preferred_element_type=F32)
+            return carry
+
+        lax.fori_loop(0, heads, own_scores, 0, unroll=4)
+
         own_prefix.wait()
         for g in gathers:
             g.wait()
         kv_t[...] = kv[...].astype(F32).T.astype(BF16)
         acc[...] = jnp.zeros_like(acc)
-        q_load.wait()
-        g_load.wait()
-
-        live = lax.broadcasted_iota(jnp.int32, (rows, hd), 0) < length
-        key_id = lax.broadcasted_iota(jnp.int32, (rows, rows), 0)
-        time_id = lax.broadcasted_iota(jnp.int32, (rows, rows), 1)
-        allowed = (key_id <= time_id) & (key_id < length)
-
         def head(h, carry):
             cols = pl.ds(pl.multiple_of(h * hd, hd), hd)
             q = qry[:, cols]
-            cot32 = jnp.where(live, gout[:, cols].astype(F32) * loss_weight, 0.0)
-            cot = cot32.astype(BF16)
-            cot_t32 = cot.astype(F32).T
-            cot_t = cot_t32.astype(BF16)
+            cot = gout[:, cols]
+            cot_t = cots_t[h]
             s_pre = lax.dot_general(kv[:prefix, :hd], q, NT, preferred_element_type=F32) * (scale * log2e)
-            s_res = lax.dot_general(kv[prefix:, :hd], q, NT, preferred_element_type=F32) * (scale * log2e)
-            s_res = jnp.where(allowed, s_res, -jnp.inf)
+            s_res = own_s[h]
             top = jnp.maximum(jnp.max(s_pre, axis=0, keepdims=True), jnp.max(s_res, axis=0, keepdims=True))
             e_pre = jnp.exp2(s_pre - top)
             e_res = jnp.exp2(s_res - top)
@@ -158,9 +168,9 @@
             out_t = jnp.dot(kv_t[hd:, :prefix], p_pre, preferred_element_type=F32) + jnp.dot(
                 kv_t[hd:, prefix:], p_res, preferred_element_type=F32)
             attn_v[:, cols] = out_t.T
-            delta = jnp.sum(cot_t32 * out_t.astype(BF16).astype(F32), axis=0, keepdims=True)
+            delta = jnp.sum(cot_t.astype(F32) * out_t.astype(BF16).astype(F32), axis=0, keepdims=True)
             d_pre = jnp.dot(kv[:prefix, hd:], cot_t, preferred_element_type=F32)
-            d_res = jnp.dot(kv[prefix:, hd:], cot_t, preferred_element_type=F32)
+            d_res = own_d[h]
             gs_pre = (f_pre * (d_pre - delta)).astype(BF16)
             gs_res = (f_res * (d_res - delta)).astype(BF16)
             gq_t = jnp.dot(kv_t[:hd, :prefix], gs_pre, preferred_element_type=F32) + jnp.dot(
@@ -259,7 +269,7 @@
                 c.start()
                 z_copies.append(c)
 
-        steps = list(range(samples - 1, -1, -1))
+        steps = sorted(range(samples), key=lambda k: (-k.bit_length(), k))
         ahead = 1
         for tick in range(samples + ahead + bits):
             if tick < samples:
@@ -320,6 +330,9 @@
         pltpu.VMEM((2, rows, 2 * hd), BF16),
         pltpu.VMEM((2, samples) + (2,) * bits + (block, hd), BF16),
         pltpu.VMEM((2, samples - 1, block, hd), BF16),
+        pltpu.VMEM((heads, hd, rows), BF16),
+        pltpu.VMEM((heads, rows, rows), F32),
+        pltpu.VMEM((heads, rows, rows), F32),
         *reduce_bufs,
         dma((2 * prompts + 2,)), dma((2,)), dma((half,)), dma((half,)),
         dma((samples,)), dma((samples,)), dma((samples,)), dma((samples,)),

time: 52.6 us -> 53.1 us (level)
    pallas_call x1, Pallas kernels: 47.9 us -> 48.4 us  [on_device(): call(hidden, queries, prefix_kv, weight, out_grad, lengths, rewards)]
where the time goes in v3:
time: 53.1 us; the launch traced here: 53 us
  Pallas kernels  51 us (96%)
  between operations  1.93 us (4%)
    pallas_call x1, Pallas kernels, on_device(): call(hidden, queries, prefix_kv, weight, out_grad, lengths, rewards)  48.4 us
    pallas_call x1, Pallas kernels, hand_out(): pl.pallas_call(kernel, out_shape=tuple((jax.ShapeDtypeStruct(a.shape, a.d...  2.61 us

profile of v3, /device:TPU:0, one launch (start us, length us, event | category | flops | bytes accessed | tf_op | source)
XLA Modules:
  0.0 53.0 jit_solution(8954250473365262994)
XLA Ops:
  1.9 48.4 %shard_map.102 = (f32[1,1,256,1024]{3,2,1,0:T(8,128)}, f32[1,1,256,1024]{3,2,1,0:T(8,128)}, f32[1,128,256]{2,1,0:T(8,128)}, f32[256,256]{1,0:T(8,128)}) custom-call(bf16[1,1,256,8192]{3,2,1,0:T(8,128)(2,1)} %hidden.1, bf16[1,1,256,1024]{3,2,1,0:T(8,128)(2,1)} %queries.1, bf16[1,128,256]{2,1,0:T(8,128)(2,1)} %prefix_in.1, bf16[8192,256]{1,0:T(8,128)(2,1)} %weight.1, ...), custom_call_target="tpu_custom_call" | custom-call | flops 4966055936 | bytes 16777216 | tf_op jit(solution)/shard_map/pallas_call | solution.py:405
  50.4 2.6 %shard_map.103 = (f32[1,1,256,1024]{3,2,1,0:T(8,128)}, f32[1,1,256,1024]{3,2,1,0:T(8,128)}, f32[1,128,256]{2,1,0:T(8,128)}, f32[256,256]{1,0:T(8,128)}) custom-call(f32[1,1,256,1024]{3,2,1,0:T(8,128)} %get-tuple-element.8.refs_0_, f32[1,1,256,1024]{3,2,1,0:T(8,128)} %get-tuple-element.9.refs_1_, f32[1,128,256]{2,1,0:T(8,128)} %get-tuple-element.10.refs_2_, ...), custom_call_target="tpu_custom_call" | custom-call | bytes 4980736 | tf_op jit(solution)/shard_map/pallas_call | solution.py:386
